TPU v7x, 512 devices: a whole 4x4x16 slice. The times are simulated.
512 devices in a mesh: dp: 32 (over x, y, core), seq: 16 (over z).
Axes of the slice: x: 4, y: 4, z: 16, core: 2. Of those that a mesh axis runs over, the one named last changes fastest.
Arguments:
- tile_tokens: bfloat16 [32, 512, 3200], P('dp', 'seq'), may hold values from -6 to 6
- proj_weight: bfloat16 [3200, 8192], P('dp', 'seq')
- text_hidden: bfloat16 [32, 2048, 8192], P('dp', 'seq'), may hold values from -6 to 6
- cotangent: bfloat16 [32, 2048, 8192], P('dp', 'seq'), may hold values from -1.1953125 to 1.1953125
- norm_gain: float32 [8192], replicated, may hold values from 0.25 to 1.75
- placeholders: int32 [32, 512], P('dp'), may hold values from 0 to 2047, as said below
- bucket_levels: int32 [32, 16, 3200], P('dp', 'seq'), may hold values from 2 to 16
- row_draws: float32 [32, 16, 3200], P('dp', 'seq'), may hold values from 0 to 1
- column_draws: float32 [32, 8192], P('dp', 'seq'), may hold values from 0 to 1
Outputs:
- weight_grad: float32 [3200, 8192], P('dp', 'seq')
- gain_grad: float32 [8192], replicated
Inputs may be any that keep to these rules, and one draw needn't show every extreme that they name: Each row is strictly increasing. Among the positions of one device's block of 128 positions stand at most 48 placeholders, and in every row some block holds exactly 48.
All inputs are finite; a program needn't handle non-finite values.
Results may differ from a plain program's by a relative error of at most 0.014.
Values may be sent and summed in bfloat16 or wider, within the bound.
A program may use at most 64 MiB of HBM per device.

v0:
```python
import jax
import jax.numpy as jnp
from jax import lax
from jax.sharding import Mesh
from jax.sharding import PartitionSpec as P

IMG_MOST = 48
DP = ("dp_0", "dp_1", "dp_2")
DP_SEQ = ("dp_0", "dp_1", "dp_2", "seq")
EPSILON = 1e-06


def copy_for_each(value, axis):
    copies = jnp.broadcast_to(value, (lax.axis_size(axis), *value.shape))
    return lax.all_to_all(copies, axis, split_axis=0, concat_axis=0, tiled=True)


def of_everyone(value, axis):
    everything = copy_for_each(value, axis)
    return jnp.sum(everything, axis=0)


def in_one(arrays, axis):
    ravelled, at, outs = (jnp.concatenate([a.reshape(-1) for a in arrays]), 0, [])
    so_far = of_everyone(ravelled, axis)
    for a in arrays:
        outs.append(so_far[at : at + a.size].reshape(a.shape))
        at += a.size
    return tuple(outs)


def one_axis_at_a_time(value, axes):
    for axis in axes:
        value = lax.psum(value, axis)
    return value


def quantize(gradient, levels_now, rows_now, columns_now):
    bucket_norm = jnp.sqrt(jnp.sum(gradient * gradient, axis=1, keepdims=True) + EPSILON)
    step_count = levels_now.astype(jnp.float32)[:, None]
    offset = 0.25 + 0.25 * (rows_now[:, None] + columns_now[None, :])
    ratio = jnp.abs(gradient) / bucket_norm * step_count
    lower = jnp.floor(ratio)
    quantum = lower + jnp.clip(2.0 * (ratio - lower - offset) + 0.5, 0.0, 1.0)
    return jnp.sign(gradient) * bucket_norm * quantum / step_count


def on_device(
    tile_tokens,
    proj_weight,
    text_hidden,
    cotangent,
    norm_gain,
    placeholders,
    bucket_levels,
    row_draws,
    column_draws,
):
    seq_count = lax.axis_size("seq")
    seq_index = lax.axis_index("seq")
    replicas = lax.axis_size(DP)
    places = placeholders[0]
    image_total = places.shape[0]
    tok_rows = text_hidden.shape[1]
    model_width = text_hidden.shape[2]
    columns = proj_weight.shape[1]
    all_positions = tok_rows * seq_count
    zero_half = jnp.zeros((), jnp.bfloat16)
    own_text = text_hidden[0]
    own_cot = cotangent[0]
    gathered = lax.all_gather(tile_tokens[0], "seq", axis=0, tiled=True)
    patch_block = gathered
    embedded = jnp.dot(
        patch_block,
        lax.all_gather(proj_weight, DP, axis=0, tiled=True),
        preferred_element_type=jnp.float32,
    ).astype(jnp.bfloat16)
    image_marks = jnp.zeros((all_positions,), jnp.int32).at[places].set(1)
    local_marks = lax.dynamic_slice_in_dim(image_marks, seq_index * tok_rows, tok_rows)
    is_image = local_marks[:, None] == 1
    owners = places // tok_rows
    owner_ids = jnp.arange(seq_count, dtype=jnp.int32)
    counts = jnp.sum((owners[:, None] == owner_ids[None, :]).astype(jnp.int32), axis=0)
    starts = jnp.cumsum(counts) - counts
    own_start = starts[seq_index]
    own_count = counts[seq_index]
    slot_ids = jnp.arange(IMG_MOST, dtype=jnp.int32)
    source_rows = jnp.clip(own_start + slot_ids, 0, image_total - 1)
    local_slots = jnp.clip(jnp.take(places, source_rows) - seq_index * tok_rows, 0, tok_rows - 1)
    slot_live = (slot_ids < own_count)[:, None]
    flat_index = owners * IMG_MOST + (
        jnp.arange(image_total, dtype=jnp.int32) - jnp.take(starts, owners)
    )
    outgoing = jnp.where(slot_live, jnp.take(own_cot, local_slots, axis=0), zero_half)
    returned = lax.all_to_all(outgoing[None], "seq", split_axis=2, concat_axis=0, tiled=True)
    image_cot = jnp.take(returned.reshape(-1, columns), flat_index, axis=0).astype(jnp.float32)
    emb_float = embedded.astype(jnp.float32)
    column_gain = lax.dynamic_slice_in_dim(norm_gain, seq_index * columns, columns)
    grad_in = image_cot * column_gain[None, :]
    squares, mixed = in_one(
        (jnp.sum(emb_float * emb_float, axis=1), jnp.sum(grad_in * emb_float, axis=1)), "seq"
    )
    inverse = lax.rsqrt(squares / model_width + EPSILON)[:, None]
    normed = emb_float * inverse
    emb_grad = ((grad_in - normed * (mixed[:, None] * inverse / model_width)) * inverse).astype(
        jnp.bfloat16
    )
    image_part = jnp.sum(image_cot * normed, axis=0)
    text_float = own_text.astype(jnp.float32)
    text_inverse = lax.rsqrt(jnp.mean(text_float * text_float, axis=1, keepdims=True) + EPSILON)
    text_terms = own_cot.astype(jnp.float32) * text_float * text_inverse
    text_part = jnp.sum(jnp.where(is_image, 0.0, text_terms), axis=0)
    placed_part = lax.dynamic_update_slice_in_dim(
        jnp.zeros((model_width,), jnp.float32), image_part, seq_index * columns, 0
    )
    gain_part = text_part + placed_part
    own_levels = bucket_levels[0, 0]
    own_row_draws = row_draws[0, 0]
    own_column_draws = column_draws[0]
    patch_block = gathered
    gradient = lax.dot_general(
        patch_block, emb_grad, (((0,), (0,)), ((), ())), preferred_element_type=jnp.float32
    )
    summed = lax.psum_scatter(
        quantize(gradient, own_levels, own_row_draws, own_column_draws).astype(jnp.bfloat16),
        DP,
        scatter_dimension=0,
        tiled=True,
    ).astype(jnp.float32)
    gain_total = one_axis_at_a_time(gain_part, DP_SEQ)
    return (summed / replicas, gain_total / replicas)


def solution(mesh):
    finer = Mesh(mesh.devices.reshape(4, 4, 2, mesh.shape["seq"]), ("dp_0", "dp_1", "dp_2", "seq"))
    return jax.shard_map(
        on_device,
        mesh=finer,
        in_specs=(
            P(DP, "seq", None),
            P(DP, "seq"),
            P(DP, "seq", None),
            P(DP, "seq", None),
            P(),
            P(DP, None),
            P(DP, "seq", None),
            P(DP, "seq", None),
            P(DP, "seq"),
        ),
        out_specs=(P(DP, "seq"), P()),
        check_vma=False,
    )
```

profile of v0, /device:TPU:6, one launch (start us, length us, event | category | flops | bytes accessed | tf_op | source)
XLA Modules:
  0.0 358.7 jit_solution(13340607720197606231)
XLA Ops:
  7.2 0.7 all-gather.7.cloned.1.call-update
  7.9 0.7 all-gather.5.cloned.1.call-update
  8.6 0.7 add_select_fusion
  9.7 0.6 dynamic_slice.12
  10.3 0.7 fusion.39
  11.1 0.7 fusion.37
  11.8 1.5 gather_fusion
  13.2 0.7 fusion.36
  13.9 3.6 %gather_fusion.1 = bf16[48,8192]{1,0:T(8,128)(2,1)S(1)} fusion(bf16[128,8192]{1,0:T(8,128)(2,1)} %bitcast.91, s32[1024]{0:T(1024)S(1)} %pad_clamp_fusion.1), kind=kCustom, calls=%fused_computation.1 | custom fusion | bytes 1573056 | tf_op jit(solution)/shard_map/jit(_take)/gather | solution.py:94
  17.6 1.3 compare_and_fusion
  18.9 0.2 fusion.25
  19.0 6.8 %copy.37 = bf16[1,48,8192]{1,0,2:T(2,128)(2,1)} copy(bf16[1,48,8192]{2,1,0:T(8,128)(2,1)S(1)} %fusion.25) | data formatting | bytes 1572864 | tf_op jit(solution)/shard_map/jit(_where)/select_n | solution.py:94
  25.9 0.5 broadcast.663
  26.4 45.1 %reduce.24 = bf16[8192,48]{1,0:T(8,128)(2,1)S(1)} reduce(bf16[8192,1,48]{2,1,0:T(2,128)(2,1)} %bitcast.93, bf16[]{:T(256)} %broadcast.663), dimensions={1}, to_apply=%bitcast.79.reduce_sub_computation | reduce | bytes 1572866
  71.5 3.9 %reshape.481 = bf16[16,2,12288]{2,1,0:T(2,128)(2,1)} reshape(bf16[8192,48]{1,0:T(8,128)(2,1)S(1)} %reduce.24) | data formatting | bytes 1572864
  75.4 15.2 %all-to-all-start = ((bf16[16,2,12288]{2,1,0:T(2,128)(2,1)}), bf16[16,2,12288]{2,1,0:T(2,128)(2,1)S(1)}, u32[]{:S(2)}, u32[]{:S(2)}) async-start(bf16[16,2,12288]{2,1,0:T(2,128)(2,1)} %reshape.481), calls=%async_computation | async-start | bytes 1572864 | tf_op jit(solution)/shard_map/all_to_all | solution.py:95
  90.6 0.8 dynamic_slice.14
  91.4 4.3 %compare_select_fusion.2 = (s32[512,1]{0,1:T(1,128)S(1)}, s32[512,1]{0,1:T(1,128)S(1)}, s32[512,1]{0,1:T(1,128)S(1)}, s32[512,1]{0,1:T(1,128)S(1)}) fusion(s32[]{:T(128)} %bitcast.12, s32[]{:T(128)} %bitcast.13, s32[]{:T(128)} %bitcast.14, s32[]{:T(128)} %bitcast.15, s32[]{:T(128)} %bitcast.16, s32[]{:T(128)} %bitcast.18, s32[]{:T(128)} %bitcast.17, ...), kind=kLoop, calls=%fused_computation.62 | loop fusion | flops 16384 | bytes 10268 | tf_op jit(solution)/shard_map/jit(_take)/gather | solution.py:92
  95.8 5.8 %compare_and_fusion.1 = (pred[512]{0:T(512)(128)(4,1)S(1)}, s32[512]{0:T(512)S(1)}) fusion(pred[512]{0:T(512)(128)(4,1)S(1)} %get-tuple-element.24, pred[512]{0:T(512)(128)(4,1)S(1)} %get-tuple-element.22, pred[512]{0:T(512)(128)(4,1)S(1)} %get-tuple-element.23, pred[512]{0:T(512)(128)(4,1)S(1)} %get-tuple-element.21, ...), kind=kLoop, calls=%fused_computation.102 | loop fusion | flops 20480 | bytes 11300 | tf_op jit(solution)/shard_map/jit(_take)/and | solution.py:96
  101.6 36.3 %all-to-all-done = bf16[16,2,12288]{2,1,0:T(2,128)(2,1)S(1)} async-done(((bf16[16,2,12288]{2,1,0:T(2,128)(2,1)}), bf16[16,2,12288]{2,1,0:T(2,128)(2,1)S(1)}, u32[]{:S(2)}, u32[]{:S(2)}) %all-to-all-start) | async-done | bytes 786464 | tf_op jit(solution)/shard_map/all_to_all | solution.py:95
  137.9 7.9 %reshape.482 = bf16[8192,1,48]{2,1,0:T(2,128)(2,1)} reshape(bf16[16,2,12288]{2,1,0:T(2,128)(2,1)S(1)} %all-to-all-done) | data formatting | bytes 1572864
  145.8 8.1 %copy.38 = bf16[1,48,8192]{2,1,0:T(8,128)(2,1)S(1)} copy(bf16[1,48,8192]{1,0,2:T(2,128)(2,1)} %bitcast.94) | data formatting | bytes 1572864 | tf_op jit(solution)/shard_map/all_to_all | solution.py:95
  154.0 0.2 copy.48
  154.3 0.4 copy.39
  154.7 2.0 gather_fusion.2
  156.7 1.0 copy.40
  157.7 3.7 %reshape.455 = bf16[3200,512]{1,0:T(8,128)(2,1)S(1)} reshape(bf16[32,100,512]{2,1,0:T(8,128)(2,1)} %all-gather.7.cloned.1.call-done) | data formatting | bytes 6553600
  161.5 19.4 %all-gather.5.cloned.1.call-done = bf16[1,512,3200]{2,1,0:T(8,128)(2,1)} async-done(((bf16[1,32,3200]{2,1,0:T(8,128)(2,1)}), bf16[1,512,3200]{2,1,0:T(8,128)(2,1)}) %all-gather.5.cloned.1.call-update) | async-done | bytes 3276816 | tf_op jit(solution)/shard_map/all_gather | solution.py:71
  180.8 4.9 %fusion.23 = (f32[512]{0:T(512)S(1)}, f32[512]{0:T(512)S(1)}, bf16[512,512]{0,1:T(8,128)(2,1)}) fusion(f32[512]{0:T(512)S(1)} %dynamic_slice.14, bf16[512,512]{0,1:T(8,128)(2,1)} %copy.40, pred[512]{0:T(512)(128)(4,1)S(1)} %get-tuple-element.25, bf16[3200,512]{1,0:T(8,128)(2,1)S(1)} %reshape.455, bf16[1,512,3200]{2,1,0:T(8,128)(2,1)} %all-gather.5.cloned.1.call-done), kind=kOutput, calls=%fused_computation.35 | convolution fusion | flops 1680079872 | bytes 7608832 | tf_op jit(solution)/shard_map/dot_general | solution.py:73
  185.7 0.7 broadcast_in_dim.90
  186.4 6.6 %all-to-all-start.1 = ((f32[16,1,1024]{2,1,0:T(1,128)}), f32[16,1,1024]{2,1,0:T(1,128)S(1)}, u32[]{:S(2)}, u32[]{:S(2)}) async-start(f32[16,1,1024]{2,1,0:T(1,128)} %broadcast_in_dim.90), calls=%async_computation.1 | async-start | bytes 131072 | tf_op jit(solution)/shard_map/all_to_all | solution.py:15
  193.1 2.7 scatter_custom_fusion
  195.8 10.0 %all-to-all-done.1 = f32[16,1,1024]{2,1,0:T(1,128)S(1)} async-done(((f32[16,1,1024]{2,1,0:T(1,128)}), f32[16,1,1024]{2,1,0:T(1,128)S(1)}, u32[]{:S(2)}, u32[]{:S(2)}) %all-to-all-start.1) | async-done | bytes 65568 | tf_op jit(solution)/shard_map/all_to_all | solution.py:15
  205.9 4.4 %multiply_reduce_fusion = (f32[3200]{0:T(1024)S(1)}, f32[512,3200]{1,0:T(8,128)S(1)}) fusion(bf16[1,512,3200]{2,1,0:T(8,128)(2,1)} %all-gather.5.cloned.1.call-done, bf16[512,512]{0,1:T(8,128)(2,1)} %get-tuple-element.50, f32[512]{0:T(512)S(1)} %get-tuple-element.31, f32[512]{0:T(512)S(1)} %get-tuple-element.30, f32[512]{0:T(512)S(1)} %dynamic_slice.14, ...), kind=kOutput, calls=%fused_computation.12 | convolution fusion | flops 1683354496 | bytes 10898432 | tf_op jit(solution)/shard_map/dot_general | solution.py:121
  210.3 6.5 %fusion.6 = bf16[3200,512]{0,1:T(8,128)(2,1)} fusion(f32[512,3200]{1,0:T(8,128)S(1)} %get-tuple-element.52, f32[3200]{0:T(1024)S(1)} %convert_reduce_fusion.1, f32[512]{0:T(512)S(1)} %bitcast.103, f32[3200]{0:T(1024)S(1)} %reduce.13, f32[3200]{0:T(1024)S(1)} %add_sqrt_fusion), kind=kLoop, calls=%fused_computation.13 | loop fusion | flops 29491200 | bytes 9870848 | tf_op jit(solution)/shard_map/convert_element_type | solution.py:125
  216.9 1.4 dynamic-slice.1
  218.9 2.1 fusion.10
  221.0 2.5 fusion.9
  223.5 0.3 fusion.22
  223.8 0.2 add_dynamic-update-slice_fusion
  224.0 14.2 %psum.28 = f32[8192]{0:T(1024)S(1)} all-reduce(f32[8192]{0:T(1024)S(1)} %add_dynamic-update-slice_fusion), channel_id=1, replica_groups=mesh['dp_0'=4,'dp_1'=4,'dp_2'=2,'seq'=16] {'dp_0'}, use_global_device_ids=true, to_apply=%region_11.12 | all-reduce | flops 8192 | bytes 65536 | tf_op jit(solution)/shard_map/psum | solution.py:34
  238.2 17.1 %psum.29 = f32[8192]{0:T(1024)S(1)} all-reduce(f32[8192]{0:T(1024)S(1)} %psum.28), channel_id=1, replica_groups=mesh['dp_0'=4,'dp_1'=4,'dp_2'=2,'seq'=16] {'dp_1'}, use_global_device_ids=true, to_apply=%region_12.13 | all-reduce | flops 8192 | bytes 65536 | tf_op jit(solution)/shard_map/psum | solution.py:34
  255.3 3.4 psum.30
  258.7 54.0 %psum.31 = f32[8192]{0:T(1024)S(1)} all-reduce(f32[8192]{0:T(1024)S(1)} %psum.30), channel_id=1, replica_groups=mesh['dp_0'=4,'dp_1'=4,'dp_2'=2,'seq'=16] {'seq'}, use_global_device_ids=true, to_apply=%region_14.15 | all-reduce | flops 8192 | bytes 65536 | tf_op jit(solution)/shard_map/psum | solution.py:34
  312.7 0.6 broadcast_multiply_fusion
  313.3 37.0 %all-reduce.3.cloned.1.call-done = bf16[3200,512]{0,1:T(8,128)(2,1)} async-done(((bf16[3200,512]{0,1:T(8,128)(2,1)}), bf16[3200,512]{0,1:T(8,128)(2,1)}) %all-reduce.3.cloned.1.call-update) | async-done | bytes 3276816
  350.3 1.1 convert_multiply_fusion.7
  351.4 0.8 copy.42
  (39 shorter events, 0.9 us)
Async XLA Ops:
  7.2 150.5 %all-gather.7.cloned.1.call-start = ((), (), s32[]{:S(2)}) async-start(), calls=%async_computation.3 | async-start | bytes 3514368 | tf_op jit(solution)/shard_map/all_gather | solution.py:75
  7.9 172.9 %all-gather.5.cloned.1.call-start = ((), (), s32[]{:S(2)}) async-start(), calls=%async_computation.2 | async-start | bytes 3481600 | tf_op jit(solution)/shard_map/all_gather | solution.py:71
  26.4 65.0 %copy-start = (s32[1,512]{1,0:T(1,128)S(1)}, s32[1,512]{1,0:T(1,128)}, u32[]{:S(2)}) copy-start(s32[1,512]{1,0:T(1,128)} %param.14) | copy-start | bytes 6148
  75.4 62.5 %all-to-all-start = ((bf16[16,2,12288]{2,1,0:T(2,128)(2,1)}), bf16[16,2,12288]{2,1,0:T(2,128)(2,1)S(1)}, u32[]{:S(2)}, u32[]{:S(2)}) async-start(bf16[16,2,12288]{2,1,0:T(2,128)(2,1)} %reshape.481), calls=%async_computation | async-start | bytes 1572864 | tf_op jit(solution)/shard_map/all_to_all | solution.py:95
  180.8 12.2 %copy-start.5 = (f32[1,1,3200]{2,1,0:T(1,128)S(1)}, f32[1,1,3200]{2,1,0:T(1,128)}, u32[]{:S(2)}) copy-start(f32[1,1,3200]{2,1,0:T(1,128)} %param.16) | copy-start | bytes 38404
  180.8 14.9 %copy-start.4 = (s32[1,1,3200]{2,1,0:T(1,128)S(1)}, s32[1,1,3200]{2,1,0:T(1,128)}, u32[]{:S(2)}) copy-start(s32[1,1,3200]{2,1,0:T(1,128)} %param.15) | copy-start | bytes 38404
  186.4 19.4 %all-to-all-start.1 = ((f32[16,1,1024]{2,1,0:T(1,128)}), f32[16,1,1024]{2,1,0:T(1,128)S(1)}, u32[]{:S(2)}, u32[]{:S(2)}) async-start(f32[16,1,1024]{2,1,0:T(1,128)} %broadcast_in_dim.90), calls=%async_computation.1 | async-start | bytes 131072 | tf_op jit(solution)/shard_map/all_to_all | solution.py:15
  193.0 157.3 %all-reduce.3.cloned.1.call-start = ((), (), s32[]{:S(2)}) async-start(), calls=%async_computation.4 | async-start | bytes 6553600
  205.9 4.4 %copy-start.6 = (f32[1,512]{1,0:T(1,128)S(1)}, f32[1,512]{1,0:T(1,128)}, u32[]{:S(2)}) copy-start(f32[1,512]{1,0:T(1,128)} %param.17) | copy-start | bytes 6148
  216.8 4.3 %copy-start.1 = (bf16[1,128,8192]{2,1,0:T(8,128)(2,1)S(1)}, bf16[1,128,8192]{2,1,0:T(8,128)(2,1)}, u32[]{:S(2)}) copy-start(bf16[1,128,8192]{2,1,0:T(8,128)(2,1)} %param.12) | copy-start | bytes 6291460
  216.8 6.8 %copy-start.2 = (bf16[512,512]{0,1:T(8,128)(2,1)S(1)}, bf16[512,512]{0,1:T(8,128)(2,1)}, u32[]{:S(2)}) copy-start(bf16[512,512]{0,1:T(8,128)(2,1)} %copy.40) | copy-start | bytes 1572868
  216.8 6.8 %copy-start.3 = (bf16[512,512]{0,1:T(8,128)(2,1)S(1)}, bf16[512,512]{0,1:T(8,128)(2,1)}, u32[]{:S(2)}) copy-start(bf16[512,512]{0,1:T(8,128)(2,1)} %get-tuple-element.50) | copy-start | bytes 1572868
Sparse Core Ops, SparseCore 0:
  11.1 64.6 all-gather.6
  77.9 102.9 all-gather.4
  216.9 133.3 all-reduce.2
where the time goes:
time: 360 us; the launch traced here: 359 us
  waiting for transfers between devices  104 us (29%)
  blocking collectives  88.7 us (25%)
  other arithmetic  72.6 us (20%)
  local copies, waits for them, and re-layouts  47.6 us (13%)
  starting transfers between devices  21.9 us (6%)
  between operations  14.7 us (4%)
  matrix products  9.27 us (3%)
    psum x4, blocking collectives, one_axis_at_a_time(): value = lax.psum(value, axis)  88.7 us
    unnamed x2, other arithmetic  45.2 us
    unnamed x4, waiting for transfers between devices  38.4 us
    all_to_all x1, waiting for transfers between devices, on_device(): lax.all_to_all(outgoing[None], 'seq', split_axis=2, concat_axis=0, tiled=...  36.3 us
    all_gather x1, waiting for transfers between devices, on_device(): gathered = lax.all_gather(tile_tokens[0], 'seq', axis=0, tiled=True)  19.4 us
    unnamed x21, local copies, waits for them, and re-layouts  18.5 us
    all_to_all x1, starting transfers between devices, on_device(): lax.all_to_all(outgoing[None], 'seq', split_axis=2, concat_axis=0, tiled=...  15.2 us
    all_to_all x1, waiting for transfers between devices, copy_for_each(): return lax.all_to_all(copies, axis, split_axis=0, concat_axis=0, tiled=True)  9.99 us
  transfers between devices with their start and end apart: 5, of which 4 were waited for; matrix products, arithmetic and copies ran while one was open for 31% of the time, Pallas kernels for 0%

commit v1 on v0

--- a/solution.py
+++ b/solution.py
@@ -8,6 +8,22 @@
 DP = ("dp_0", "dp_1", "dp_2")
 DP_SEQ = ("dp_0", "dp_1", "dp_2", "seq")
 EPSILON = 1e-06
+
+
+def swapped_with_each(array, axis, split, join):
+    ways, here = (lax.axis_size(axis), lax.axis_index(axis))
+    width = array.shape[split] // ways
+    shape = list(array.shape)
+    shape[split] = width
+    height = shape[join]
+    shape[join] = height * ways
+    full = jnp.zeros(shape, array.dtype)
+    for mask in range(ways):
+        part = lax.dynamic_slice_in_dim(array, (here ^ mask) * width, width, axis=split)
+        if mask:
+            part = lax.ppermute(part, axis, [(d, d ^ mask) for d in range(ways)])
+        full = lax.dynamic_update_slice_in_dim(full, part, (here ^ mask) * height, axis=join)
+    return full
 
 
 def copy_for_each(value, axis):
@@ -92,7 +108,7 @@
         jnp.arange(image_total, dtype=jnp.int32) - jnp.take(starts, owners)
     )
     outgoing = jnp.where(slot_live, jnp.take(own_cot, local_slots, axis=0), zero_half)
-    returned = lax.all_to_all(outgoing[None], "seq", split_axis=2, concat_axis=0, tiled=True)
+    returned = swapped_with_each(outgoing[None], "seq", 2, 0)
     image_cot = jnp.take(returned.reshape(-1, columns), flat_index, axis=0).astype(jnp.float32)
     emb_float = embedded.astype(jnp.float32)
     column_gain = lax.dynamic_slice_in_dim(norm_gain, seq_index * columns, columns)

time: 360 us -> 347 us (0.964)
  starting transfers between devices: 21.9 us -> 89.1 us
  other arithmetic: 72.6 us -> 27.4 us
  local copies, waits for them, and re-layouts: 47.6 us -> 19.8 us
  waiting for transfers between devices: 104 us -> 96 us
    ppermute x0 -> x15, starting transfers between devices: none -> 81.8 us  [swapped_with_each(): part = lax.ppermute(part, axis, [(d, d ^ mask) for d in range(ways)])]
    unnamed x2 -> x1, other arithmetic: 45.2 us -> 0.04 us
    all_to_all x1 -> x0, waiting for transfers between devices: 36.3 us -> none  [on_device(): lax.all_to_all(outgoing[None], 'seq', split_axis=2, concat_axis=0, tiled=...]
    all_gather x1, waiting for transfers between devices: 19.4 us -> 38.6 us  [on_device(): gathered = lax.all_gather(tile_tokens[0], 'seq', axis=0, tiled=True)]
    all_to_all x1 -> x0, starting transfers between devices: 15.2 us -> none  [on_device(): lax.all_to_all(outgoing[None], 'seq', split_axis=2, concat_axis=0, tiled=...]
    unnamed x21 -> x17, local copies, waits for them, and re-layouts: 18.5 us -> 5.94 us
    ppermute x0 -> x15, waiting for transfers between devices: none -> 9.14 us  [swapped_with_each(): part = lax.ppermute(part, axis, [(d, d ^ mask) for d in range(ways)])]
    all_to_all x3 -> x0, local copies, waits for them, and re-layouts: 8.62 us -> none  [on_device(): lax.all_to_all(outgoing[None], 'seq', split_axis=2, concat_axis=0, tiled=...]
  transfers between devices with their start and end apart: 5 -> 19, of which waited for: 4 -> 5; matrix products, arithmetic and copies ran while one was open for 31% -> 11% of each run, Pallas kernels for 0% -> 0%
where the time goes in v1:
time: 347 us; the launch traced here: 346 us
  waiting for transfers between devices  96 us (28%)
  starting transfers between devices  89.1 us (26%)
  blocking collectives  88.8 us (26%)
  other arithmetic  27.4 us (8%)
  local copies, waits for them, and re-layouts  19.8 us (6%)
  between operations  15.3 us (4%)
  matrix products  9.25 us (3%)
    psum x4, blocking collectives, one_axis_at_a_time(): value = lax.psum(value, axis)  88.8 us
    ppermute x15, starting transfers between devices, swapped_with_each(): part = lax.ppermute(part, axis, [(d, d ^ mask) for d in range(ways)])  81.8 us
    all_gather x1, waiting for transfers between devices, on_device(): gathered = lax.all_gather(tile_tokens[0], 'seq', axis=0, tiled=True)  38.6 us
    unnamed x4, waiting for transfers between devices  38.3 us
    all_to_all x1, waiting for transfers between devices, copy_for_each(): return lax.all_to_all(copies, axis, split_axis=0, concat_axis=0, tiled=True)  10 us
    ppermute x15, waiting for transfers between devices, swapped_with_each(): part = lax.ppermute(part, axis, [(d, d ^ mask) for d in range(ways)])  9.14 us
    all_to_all x1, starting transfers between devices, copy_for_each(): return lax.all_to_all(copies, axis, split_axis=0, concat_axis=0, tiled=True)  7.17 us
  transfers between devices with their start and end apart: 19, of which 5 were waited for; matrix products, arithmetic and copies ran while one was open for 11% of the time, Pallas kernels for 0%

profile of v1, /device:TPU:6, one launch (start us, length us, event | category | flops | bytes accessed | tf_op | source)
XLA Modules:
  0.0 345.6 jit_solution(13072340814138610611)
XLA Ops:
  7.2 0.7 all-gather.7.cloned.1.call-update
  8.0 0.7 all-gather.5.cloned.1.call-update
  8.7 0.7 add_select_fusion
  10.4 0.7 fusion.38
  11.8 1.5 gather_fusion
  13.3 0.7 fusion.35
  14.0 3.6 %gather_fusion.1 = bf16[48,8192]{1,0:T(8,128)(2,1)S(1)} fusion(bf16[128,8192]{1,0:T(8,128)(2,1)} %bitcast.109, s32[1024]{0:T(1024)S(1)} %pad_clamp_fusion.1), kind=kCustom, calls=%fused_computation.1 | custom fusion | bytes 1573056 | tf_op jit(solution)/shard_map/jit(_take)/gather | solution.py:110
  17.7 1.3 compare_and_fusion
  19.4 3.8 %collective-permute-start = (bf16[1,48,512]{2,1,0:T(8,128)(2,1)S(1)}, bf16[1,48,512]{2,1,0:T(8,128)(2,1)S(1)}, u32[]{:S(2)}, u32[]{:S(2)}) collective-permute-start(bf16[1,48,512]{2,1,0:T(8,128)(2,1)S(1)} %get-tuple-element.42), channel_id=1, source_target_pairs={{0,1},{1,0},{2,3},{3,2},{4,5},{5,4},{6,7},{7,6},{8,9},{9,8},{10,11... | collective-permute-start | bytes 147464 | tf_op jit(solution)/shard_map/ppermute | solution.py:24
  23.2 5.2 %collective-permute-start.1 = (bf16[1,48,512]{2,1,0:T(8,128)(2,1)S(1)}, bf16[1,48,512]{2,1,0:T(8,128)(2,1)S(1)}, u32[]{:S(2)}, u32[]{:S(2)}) collective-permute-start(bf16[1,48,512]{2,1,0:T(8,128)(2,1)S(1)} %get-tuple-element.41), channel_id=1, source_target_pairs={{0,2},{1,3},{2,0},{3,1},{4,6},{5,7},{6,4},{7,5},{8,10},{9,11},{10,... | collective-permute-start | bytes 147464 | tf_op jit(solution)/shard_map/ppermute | solution.py:24
  28.4 1.9 collective-permute-start.2
  30.3 9.1 %collective-permute-start.3 = (bf16[1,48,512]{2,1,0:T(8,128)(2,1)S(1)}, bf16[1,48,512]{2,1,0:T(8,128)(2,1)S(1)}, u32[]{:S(2)}, u32[]{:S(2)}) collective-permute-start(bf16[1,48,512]{2,1,0:T(8,128)(2,1)S(1)} %get-tuple-element.39), channel_id=1, source_target_pairs={{0,4},{1,5},{2,6},{3,7},{4,0},{5,1},{6,2},{7,3},{8,12},{9,13},{10,... | collective-permute-start | bytes 147464 | tf_op jit(solution)/shard_map/ppermute | solution.py:24
  39.4 1.9 collective-permute-start.4
  41.5 4.3 %compare_select_fusion.2 = (s32[512,1]{0,1:T(1,128)S(1)}, s32[512,1]{0,1:T(1,128)S(1)}, s32[512,1]{0,1:T(1,128)S(1)}, s32[512,1]{0,1:T(1,128)S(1)}) fusion(s32[]{:T(128)} %bitcast.12, s32[]{:T(128)} %bitcast.13, s32[]{:T(128)} %bitcast.14, s32[]{:T(128)} %bitcast.15, s32[]{:T(128)} %bitcast.16, s32[]{:T(128)} %bitcast.18, s32[]{:T(128)} %bitcast.17, ...), kind=kLoop, calls=%fused_computation.91 | loop fusion | flops 16384 | bytes 10268 | tf_op jit(solution)/shard_map/jit(_take)/gather | solution.py:108
  45.8 5.8 %compare_and_fusion.1 = (pred[512]{0:T(512)(128)(4,1)S(1)}, s32[512]{0:T(512)S(1)}) fusion(pred[512]{0:T(512)(128)(4,1)S(1)} %get-tuple-element.22, pred[512]{0:T(512)(128)(4,1)S(1)} %get-tuple-element.20, pred[512]{0:T(512)(128)(4,1)S(1)} %get-tuple-element.21, pred[512]{0:T(512)(128)(4,1)S(1)} %get-tuple-element.19, ...), kind=kLoop, calls=%fused_computation.131 | loop fusion | flops 20480 | bytes 11300 | tf_op jit(solution)/shard_map/jit(_take)/and | solution.py:112
  51.8 0.8 dynamic_slice.78
  52.5 10.2 %collective-permute-start.5 = (bf16[1,48,512]{2,1,0:T(8,128)(2,1)S(1)}, bf16[1,48,512]{2,1,0:T(8,128)(2,1)S(1)}, u32[]{:S(2)}, u32[]{:S(2)}) collective-permute-start(bf16[1,48,512]{2,1,0:T(8,128)(2,1)S(1)} %get-tuple-element.37), channel_id=1, source_target_pairs={{0,6},{1,7},{2,4},{3,5},{4,2},{5,3},{6,0},{7,1},{8,14},{9,15},{10,... | collective-permute-start | bytes 147464 | tf_op jit(solution)/shard_map/ppermute | solution.py:24
  62.7 1.9 collective-permute-start.6
  64.7 13.1 %collective-permute-start.7 = (bf16[1,48,512]{2,1,0:T(8,128)(2,1)S(1)}, bf16[1,48,512]{2,1,0:T(8,128)(2,1)S(1)}, u32[]{:S(2)}, u32[]{:S(2)}) collective-permute-start(bf16[1,48,512]{2,1,0:T(8,128)(2,1)S(1)} %get-tuple-element.35), channel_id=1, source_target_pairs={{0,8},{1,9},{2,10},{3,11},{4,12},{5,13},{6,14},{7,15},{8,0},{9,1},... | collective-permute-start | bytes 147464 | tf_op jit(solution)/shard_map/ppermute | solution.py:24
  77.8 1.9 collective-permute-start.8
  79.8 7.7 %collective-permute-start.9 = (bf16[1,48,512]{2,1,0:T(8,128)(2,1)S(1)}, bf16[1,48,512]{2,1,0:T(8,128)(2,1)S(1)}, u32[]{:S(2)}, u32[]{:S(2)}) collective-permute-start(bf16[1,48,512]{2,1,0:T(8,128)(2,1)S(1)} %get-tuple-element.33), channel_id=1, source_target_pairs={{0,10},{1,11},{2,8},{3,9},{4,14},{5,15},{6,12},{7,13},{8,2},{9,3},... | collective-permute-start | bytes 147464 | tf_op jit(solution)/shard_map/ppermute | solution.py:24
  87.5 4.2 %collective-permute-start.10 = (bf16[1,48,512]{2,1,0:T(8,128)(2,1)S(1)}, bf16[1,48,512]{2,1,0:T(8,128)(2,1)S(1)}, u32[]{:S(2)}, u32[]{:S(2)}) collective-permute-start(bf16[1,48,512]{2,1,0:T(8,128)(2,1)S(1)} %get-tuple-element.32), channel_id=1, source_target_pairs={{0,11},{1,10},{2,9},{3,8},{4,15},{5,14},{6,13},{7,12},{8,3},{9,2},... | collective-permute-start | bytes 147464 | tf_op jit(solution)/shard_map/ppermute | solution.py:24
  91.7 6.1 %collective-permute-start.11 = (bf16[1,48,512]{2,1,0:T(8,128)(2,1)S(1)}, bf16[1,48,512]{2,1,0:T(8,128)(2,1)S(1)}, u32[]{:S(2)}, u32[]{:S(2)}) collective-permute-start(bf16[1,48,512]{2,1,0:T(8,128)(2,1)S(1)} %get-tuple-element.31), channel_id=1, source_target_pairs={{0,12},{1,13},{2,14},{3,15},{4,8},{5,9},{6,10},{7,11},{8,4},{9,5},... | collective-permute-start | bytes 147464 | tf_op jit(solution)/shard_map/ppermute | solution.py:24
  97.8 4.6 %collective-permute-start.12 = (bf16[1,48,512]{2,1,0:T(8,128)(2,1)S(1)}, bf16[1,48,512]{2,1,0:T(8,128)(2,1)S(1)}, u32[]{:S(2)}, u32[]{:S(2)}) collective-permute-start(bf16[1,48,512]{2,1,0:T(8,128)(2,1)S(1)} %get-tuple-element.30), channel_id=1, source_target_pairs={{0,13},{1,12},{2,15},{3,14},{4,9},{5,8},{6,11},{7,10},{8,5},{9,4},... | collective-permute-start | bytes 147464 | tf_op jit(solution)/shard_map/ppermute | solution.py:24
  102.4 8.3 %collective-permute-start.13 = (bf16[1,48,512]{2,1,0:T(8,128)(2,1)S(1)}, bf16[1,48,512]{2,1,0:T(8,128)(2,1)S(1)}, u32[]{:S(2)}, u32[]{:S(2)}) collective-permute-start(bf16[1,48,512]{2,1,0:T(8,128)(2,1)S(1)} %get-tuple-element.29), channel_id=1, source_target_pairs={{0,14},{1,15},{2,12},{3,13},{4,10},{5,11},{6,8},{7,9},{8,6},{9,7},... | collective-permute-start | bytes 147464 | tf_op jit(solution)/shard_map/ppermute | solution.py:24
  110.8 1.9 collective-permute-start.14
  112.8 3.5 %collective-permute-done.13 = bf16[1,48,512]{2,1,0:T(8,128)(2,1)S(1)} collective-permute-done((bf16[1,48,512]{2,1,0:T(8,128)(2,1)S(1)}, bf16[1,48,512]{2,1,0:T(8,128)(2,1)S(1)}, u32[]{:S(2)}, u32[]{:S(2)}) %collective-permute-start.13) | collective-permute-done | bytes 49184 | tf_op jit(solution)/shard_map/ppermute | solution.py:24
  116.3 5.6 %collective-permute-done.14 = bf16[1,48,512]{2,1,0:T(8,128)(2,1)S(1)} collective-permute-done((bf16[1,48,512]{2,1,0:T(8,128)(2,1)S(1)}, bf16[1,48,512]{2,1,0:T(8,128)(2,1)S(1)}, u32[]{:S(2)}, u32[]{:S(2)}) %collective-permute-start.14) | collective-permute-done | bytes 49184 | tf_op jit(solution)/shard_map/ppermute | solution.py:24
  122.0 2.0 gather_fusion.2
  123.9 1.0 copy.24
  124.9 3.7 %reshape.425 = bf16[3200,512]{1,0:T(8,128)(2,1)S(1)} reshape(bf16[32,100,512]{2,1,0:T(8,128)(2,1)} %all-gather.7.cloned.1.call-done) | data formatting | bytes 6553600
  128.7 38.6 %all-gather.5.cloned.1.call-done = bf16[1,512,3200]{2,1,0:T(8,128)(2,1)} async-done(((bf16[1,32,3200]{2,1,0:T(8,128)(2,1)}), bf16[1,512,3200]{2,1,0:T(8,128)(2,1)}) %all-gather.5.cloned.1.call-update) | async-done | bytes 3276816 | tf_op jit(solution)/shard_map/all_gather | solution.py:87
  167.3 4.9 %fusion.23 = (f32[512]{0:T(512)S(1)}, f32[512]{0:T(512)S(1)}, bf16[512,512]{0,1:T(8,128)(2,1)}) fusion(f32[512]{0:T(512)S(1)} %dynamic_slice.78, bf16[512,512]{0,1:T(8,128)(2,1)} %copy.24, pred[512]{0:T(512)(128)(4,1)S(1)} %get-tuple-element.23, bf16[3200,512]{1,0:T(8,128)(2,1)S(1)} %reshape.425, bf16[1,512,3200]{2,1,0:T(8,128)(2,1)} %all-gather.5.cloned.1.call-done), kind=kOutput, calls=%fused_computation.35 | convolution fusion | flops 1680079872 | bytes 7608832 | tf_op jit(solution)/shard_map/dot_general | solution.py:89
  172.8 7.2 %all-to-all-start = ((f32[16,1,1024]{2,1,0:T(1,128)}), f32[16,1,1024]{2,1,0:T(1,128)S(1)}, u32[]{:S(2)}, u32[]{:S(2)}) async-start(f32[16,1,1024]{2,1,0:T(1,128)} %broadcast_in_dim.94), calls=%async_computation | async-start | bytes 131072 | tf_op jit(solution)/shard_map/all_to_all | solution.py:31
  180.1 2.6 scatter_custom_fusion
  182.8 10.0 %all-to-all-done = f32[16,1,1024]{2,1,0:T(1,128)S(1)} async-done(((f32[16,1,1024]{2,1,0:T(1,128)}), f32[16,1,1024]{2,1,0:T(1,128)S(1)}, u32[]{:S(2)}, u32[]{:S(2)}) %all-to-all-start) | async-done | bytes 65568 | tf_op jit(solution)/shard_map/all_to_all | solution.py:31
  192.9 4.4 %multiply_reduce_fusion = (f32[3200]{0:T(1024)S(1)}, f32[512,3200]{1,0:T(8,128)S(1)}) fusion(bf16[1,512,3200]{2,1,0:T(8,128)(2,1)} %all-gather.5.cloned.1.call-done, bf16[512,512]{0,1:T(8,128)(2,1)} %get-tuple-element.63, f32[512]{0:T(512)S(1)} %get-tuple-element.44, f32[512]{0:T(512)S(1)} %get-tuple-element.43, f32[512]{0:T(512)S(1)} %dynamic_slice.78, ...), kind=kOutput, calls=%fused_computation.12 | convolution fusion | flops 1683354496 | bytes 10898432 | tf_op jit(solution)/shard_map/dot_general | solution.py:137
  197.3 6.4 %fusion.6 = bf16[3200,512]{0,1:T(8,128)(2,1)} fusion(f32[512,3200]{1,0:T(8,128)S(1)} %get-tuple-element.65, f32[3200]{0:T(1024)S(1)} %convert_reduce_fusion.1, f32[512]{0:T(512)S(1)} %bitcast.117, f32[3200]{0:T(1024)S(1)} %reduce.13, f32[3200]{0:T(1024)S(1)} %add_sqrt_fusion), kind=kLoop, calls=%fused_computation.13 | loop fusion | flops 29491200 | bytes 9870848 | tf_op jit(solution)/shard_map/convert_element_type | solution.py:141
  203.9 1.3 dynamic-slice.65
  205.9 2.1 fusion.10
  208.0 2.5 fusion.9
  210.9 14.1 %psum.28 = f32[8192]{0:T(1024)S(1)} all-reduce(f32[8192]{0:T(1024)S(1)} %add_dynamic-update-slice_fusion), channel_id=1, replica_groups=mesh['dp_0'=4,'dp_1'=4,'dp_2'=2,'seq'=16] {'dp_0'}, use_global_device_ids=true, to_apply=%region_11.12 | all-reduce | flops 8192 | bytes 65536 | tf_op jit(solution)/shard_map/psum | solution.py:50
  225.0 17.4 %psum.29 = f32[8192]{0:T(1024)S(1)} all-reduce(f32[8192]{0:T(1024)S(1)} %psum.28), channel_id=1, replica_groups=mesh['dp_0'=4,'dp_1'=4,'dp_2'=2,'seq'=16] {'dp_1'}, use_global_device_ids=true, to_apply=%region_12.13 | all-reduce | flops 8192 | bytes 65536 | tf_op jit(solution)/shard_map/psum | solution.py:50
  242.5 3.4 psum.30
  245.9 53.8 %psum.31 = f32[8192]{0:T(1024)S(1)} all-reduce(f32[8192]{0:T(1024)S(1)} %psum.30), channel_id=1, replica_groups=mesh['dp_0'=4,'dp_1'=4,'dp_2'=2,'seq'=16] {'seq'}, use_global_device_ids=true, to_apply=%region_14.15 | all-reduce | flops 8192 | bytes 65536 | tf_op jit(solution)/shard_map/psum | solution.py:50
  300.3 36.9 %all-reduce.3.cloned.1.call-done = bf16[3200,512]{0,1:T(8,128)(2,1)} async-done(((bf16[3200,512]{0,1:T(8,128)(2,1)}), bf16[3200,512]{0,1:T(8,128)(2,1)}) %all-reduce.3.cloned.1.call-update) | async-done | bytes 3276816
  337.2 1.1 convert_multiply_fusion.7
  338.3 0.8 copy.26
  (76 shorter events, 4.5 us)
Async XLA Ops:
  7.2 34.3 %copy-start = (s32[1,512]{1,0:T(1,128)S(1)}, s32[1,512]{1,0:T(1,128)}, u32[]{:S(2)}) copy-start(s32[1,512]{1,0:T(1,128)} %param.14) | copy-start | bytes 6148
  7.2 117.8 %all-gather.7.cloned.1.call-start = ((), (), s32[]{:S(2)}) async-start(), calls=%async_computation.2 | async-start | bytes 3514368 | tf_op jit(solution)/shard_map/all_gather | solution.py:91
  7.9 159.4 %all-gather.5.cloned.1.call-start = ((), (), s32[]{:S(2)}) async-start(), calls=%async_computation.1 | async-start | bytes 3481600 | tf_op jit(solution)/shard_map/all_gather | solution.py:87
  19.4 33.2 %collective-permute-start = (bf16[1,48,512]{2,1,0:T(8,128)(2,1)S(1)}, bf16[1,48,512]{2,1,0:T(8,128)(2,1)S(1)}, u32[]{:S(2)}, u32[]{:S(2)}) collective-permute-start(bf16[1,48,512]{2,1,0:T(8,128)(2,1)S(1)} %get-tuple-element.42), channel_id=1, source_target_pairs={{0,1},{1,0},{2,3},{3,2},{4,5},{5,4},{6,7},{7,6},{8,9},{9,8},{10,11... | collective-permute-start | bytes 147464 | tf_op jit(solution)/shard_map/ppermute | solution.py:24
  23.2 39.5 %collective-permute-start.1 = (bf16[1,48,512]{2,1,0:T(8,128)(2,1)S(1)}, bf16[1,48,512]{2,1,0:T(8,128)(2,1)S(1)}, u32[]{:S(2)}, u32[]{:S(2)}) collective-permute-start(bf16[1,48,512]{2,1,0:T(8,128)(2,1)S(1)} %get-tuple-element.41), channel_id=1, source_target_pairs={{0,2},{1,3},{2,0},{3,1},{4,6},{5,7},{6,4},{7,5},{8,10},{9,11},{10,... | collective-permute-start | bytes 147464 | tf_op jit(solution)/shard_map/ppermute | solution.py:24
  28.4 36.3 %collective-permute-start.2 = (bf16[1,48,512]{2,1,0:T(8,128)(2,1)S(1)}, bf16[1,48,512]{2,1,0:T(8,128)(2,1)S(1)}, u32[]{:S(2)}, u32[]{:S(2)}) collective-permute-start(bf16[1,48,512]{2,1,0:T(8,128)(2,1)S(1)} %get-tuple-element.40), channel_id=1, source_target_pairs={{0,3},{1,2},{2,1},{3,0},{4,7},{5,6},{6,5},{7,4},{8,11},{9,10},{10,... | collective-permute-start | bytes 147464 | tf_op jit(solution)/shard_map/ppermute | solution.py:24
  30.3 47.5 %collective-permute-start.3 = (bf16[1,48,512]{2,1,0:T(8,128)(2,1)S(1)}, bf16[1,48,512]{2,1,0:T(8,128)(2,1)S(1)}, u32[]{:S(2)}, u32[]{:S(2)}) collective-permute-start(bf16[1,48,512]{2,1,0:T(8,128)(2,1)S(1)} %get-tuple-element.39), channel_id=1, source_target_pairs={{0,4},{1,5},{2,6},{3,7},{4,0},{5,1},{6,2},{7,3},{8,12},{9,13},{10,... | collective-permute-start | bytes 147464 | tf_op jit(solution)/shard_map/ppermute | solution.py:24
  39.4 40.4 %collective-permute-start.4 = (bf16[1,48,512]{2,1,0:T(8,128)(2,1)S(1)}, bf16[1,48,512]{2,1,0:T(8,128)(2,1)S(1)}, u32[]{:S(2)}, u32[]{:S(2)}) collective-permute-start(bf16[1,48,512]{2,1,0:T(8,128)(2,1)S(1)} %get-tuple-element.38), channel_id=1, source_target_pairs={{0,5},{1,4},{2,7},{3,6},{4,1},{5,0},{6,3},{7,2},{8,13},{9,12},{10,... | collective-permute-start | bytes 147464 | tf_op jit(solution)/shard_map/ppermute | solution.py:24
  52.5 35.0 %collective-permute-start.5 = (bf16[1,48,512]{2,1,0:T(8,128)(2,1)S(1)}, bf16[1,48,512]{2,1,0:T(8,128)(2,1)S(1)}, u32[]{:S(2)}, u32[]{:S(2)}) collective-permute-start(bf16[1,48,512]{2,1,0:T(8,128)(2,1)S(1)} %get-tuple-element.37), channel_id=1, source_target_pairs={{0,6},{1,7},{2,4},{3,5},{4,2},{5,3},{6,0},{7,1},{8,14},{9,15},{10,... | collective-permute-start | bytes 147464 | tf_op jit(solution)/shard_map/ppermute | solution.py:24
  62.7 29.0 %collective-permute-start.6 = (bf16[1,48,512]{2,1,0:T(8,128)(2,1)S(1)}, bf16[1,48,512]{2,1,0:T(8,128)(2,1)S(1)}, u32[]{:S(2)}, u32[]{:S(2)}) collective-permute-start(bf16[1,48,512]{2,1,0:T(8,128)(2,1)S(1)} %get-tuple-element.36), channel_id=1, source_target_pairs={{0,7},{1,6},{2,5},{3,4},{4,3},{5,2},{6,1},{7,0},{8,15},{9,14},{10,... | collective-permute-start | bytes 147464 | tf_op jit(solution)/shard_map/ppermute | solution.py:24
  64.7 33.1 %collective-permute-start.7 = (bf16[1,48,512]{2,1,0:T(8,128)(2,1)S(1)}, bf16[1,48,512]{2,1,0:T(8,128)(2,1)S(1)}, u32[]{:S(2)}, u32[]{:S(2)}) collective-permute-start(bf16[1,48,512]{2,1,0:T(8,128)(2,1)S(1)} %get-tuple-element.35), channel_id=1, source_target_pairs={{0,8},{1,9},{2,10},{3,11},{4,12},{5,13},{6,14},{7,15},{8,0},{9,1},... | collective-permute-start | bytes 147464 | tf_op jit(solution)/shard_map/ppermute | solution.py:24
  77.8 24.6 %collective-permute-start.8 = (bf16[1,48,512]{2,1,0:T(8,128)(2,1)S(1)}, bf16[1,48,512]{2,1,0:T(8,128)(2,1)S(1)}, u32[]{:S(2)}, u32[]{:S(2)}) collective-permute-start(bf16[1,48,512]{2,1,0:T(8,128)(2,1)S(1)} %get-tuple-element.34), channel_id=1, source_target_pairs={{0,9},{1,8},{2,11},{3,10},{4,13},{5,12},{6,15},{7,14},{8,1},{9,0},... | collective-permute-start | bytes 147464 | tf_op jit(solution)/shard_map/ppermute | solution.py:24
  79.8 31.0 %collective-permute-start.9 = (bf16[1,48,512]{2,1,0:T(8,128)(2,1)S(1)}, bf16[1,48,512]{2,1,0:T(8,128)(2,1)S(1)}, u32[]{:S(2)}, u32[]{:S(2)}) collective-permute-start(bf16[1,48,512]{2,1,0:T(8,128)(2,1)S(1)} %get-tuple-element.33), channel_id=1, source_target_pairs={{0,10},{1,11},{2,8},{3,9},{4,14},{5,15},{6,12},{7,13},{8,2},{9,3},... | collective-permute-start | bytes 147464 | tf_op jit(solution)/shard_map/ppermute | solution.py:24
  87.5 25.2 %collective-permute-start.10 = (bf16[1,48,512]{2,1,0:T(8,128)(2,1)S(1)}, bf16[1,48,512]{2,1,0:T(8,128)(2,1)S(1)}, u32[]{:S(2)}, u32[]{:S(2)}) collective-permute-start(bf16[1,48,512]{2,1,0:T(8,128)(2,1)S(1)} %get-tuple-element.32), channel_id=1, source_target_pairs={{0,11},{1,10},{2,9},{3,8},{4,15},{5,14},{6,13},{7,12},{8,3},{9,2},... | collective-permute-start | bytes 147464 | tf_op jit(solution)/shard_map/ppermute | solution.py:24
  91.7 21.1 %collective-permute-start.11 = (bf16[1,48,512]{2,1,0:T(8,128)(2,1)S(1)}, bf16[1,48,512]{2,1,0:T(8,128)(2,1)S(1)}, u32[]{:S(2)}, u32[]{:S(2)}) collective-permute-start(bf16[1,48,512]{2,1,0:T(8,128)(2,1)S(1)} %get-tuple-element.31), channel_id=1, source_target_pairs={{0,12},{1,13},{2,14},{3,15},{4,8},{5,9},{6,10},{7,11},{8,4},{9,5},... | collective-permute-start | bytes 147464 | tf_op jit(solution)/shard_map/ppermute | solution.py:24
  97.8 15.0 %collective-permute-start.12 = (bf16[1,48,512]{2,1,0:T(8,128)(2,1)S(1)}, bf16[1,48,512]{2,1,0:T(8,128)(2,1)S(1)}, u32[]{:S(2)}, u32[]{:S(2)}) collective-permute-start(bf16[1,48,512]{2,1,0:T(8,128)(2,1)S(1)} %get-tuple-element.30), channel_id=1, source_target_pairs={{0,13},{1,12},{2,15},{3,14},{4,9},{5,8},{6,11},{7,10},{8,5},{9,4},... | collective-permute-start | bytes 147464 | tf_op jit(solution)/shard_map/ppermute | solution.py:24
  102.4 13.9 %collective-permute-start.13 = (bf16[1,48,512]{2,1,0:T(8,128)(2,1)S(1)}, bf16[1,48,512]{2,1,0:T(8,128)(2,1)S(1)}, u32[]{:S(2)}, u32[]{:S(2)}) collective-permute-start(bf16[1,48,512]{2,1,0:T(8,128)(2,1)S(1)} %get-tuple-element.29), channel_id=1, source_target_pairs={{0,14},{1,15},{2,12},{3,13},{4,10},{5,11},{6,8},{7,9},{8,6},{9,7},... | collective-permute-start | bytes 147464 | tf_op jit(solution)/shard_map/ppermute | solution.py:24
  110.8 11.2 %collective-permute-start.14 = (bf16[1,48,512]{2,1,0:T(8,128)(2,1)S(1)}, bf16[1,48,512]{2,1,0:T(8,128)(2,1)S(1)}, u32[]{:S(2)}, u32[]{:S(2)}) collective-permute-start(bf16[1,48,512]{2,1,0:T(8,128)(2,1)S(1)} %get-tuple-element.28), channel_id=1, source_target_pairs={{0,15},{1,14},{2,13},{3,12},{4,11},{5,10},{6,9},{7,8},{8,7},{9,6},... | collective-permute-start | bytes 147464 | tf_op jit(solution)/shard_map/ppermute | solution.py:24
  128.7 51.4 %copy-start.5 = (f32[1,1,3200]{2,1,0:T(1,128)S(1)}, f32[1,1,3200]{2,1,0:T(1,128)}, u32[]{:S(2)}) copy-start(f32[1,1,3200]{2,1,0:T(1,128)} %param.16) | copy-start | bytes 38404
  128.7 54.1 %copy-start.4 = (s32[1,1,3200]{2,1,0:T(1,128)S(1)}, s32[1,1,3200]{2,1,0:T(1,128)}, u32[]{:S(2)}) copy-start(s32[1,1,3200]{2,1,0:T(1,128)} %param.15) | copy-start | bytes 38404
  172.2 25.2 %copy-start.6 = (f32[1,512]{1,0:T(1,128)S(1)}, f32[1,512]{1,0:T(1,128)}, u32[]{:S(2)}) copy-start(f32[1,512]{1,0:T(1,128)} %param.17) | copy-start | bytes 6148
  172.8 20.0 %all-to-all-start = ((f32[16,1,1024]{2,1,0:T(1,128)}), f32[16,1,1024]{2,1,0:T(1,128)S(1)}, u32[]{:S(2)}, u32[]{:S(2)}) async-start(f32[16,1,1024]{2,1,0:T(1,128)} %broadcast_in_dim.94), calls=%async_computation | async-start | bytes 131072 | tf_op jit(solution)/shard_map/all_to_all | solution.py:31
  180.0 157.2 %all-reduce.3.cloned.1.call-start = ((), (), s32[]{:S(2)}) async-start(), calls=%async_computation.3 | async-start | bytes 6553600
  197.3 10.6 %copy-start.1 = (bf16[1,128,8192]{2,1,0:T(8,128)(2,1)S(1)}, bf16[1,128,8192]{2,1,0:T(8,128)(2,1)}, u32[]{:S(2)}) copy-start(bf16[1,128,8192]{2,1,0:T(8,128)(2,1)} %param.12) | copy-start | bytes 6291460
  203.8 6.7 %copy-start.2 = (bf16[512,512]{0,1:T(8,128)(2,1)S(1)}, bf16[512,512]{0,1:T(8,128)(2,1)}, u32[]{:S(2)}) copy-start(bf16[512,512]{0,1:T(8,128)(2,1)} %copy.24) | copy-start | bytes 1572868
  203.8 6.7 %copy-start.3 = (bf16[512,512]{0,1:T(8,128)(2,1)S(1)}, bf16[512,512]{0,1:T(8,128)(2,1)}, u32[]{:S(2)}) copy-start(bf16[512,512]{0,1:T(8,128)(2,1)} %get-tuple-element.63) | copy-start | bytes 1572868
Sparse Core Ops, SparseCore 0:
  11.1 64.6 all-gather.6
  77.9 89.3 all-gather.4
  203.9 133.2 all-reduce.2
